TPU v7x, 512 devices: a whole 4x4x16 slice. The times are simulated.
512 devices in a mesh: replica: 64 (over x, z_hi, y, core), tp: 8 (over z_lo).
Axes of the slice: x: 4, y: 4, z: 16 (z_hi: 2, z_lo: 8; z = z_hi * 8 + z_lo), core: 2. Of those that a mesh axis runs over, the one named last changes fastest.
Arguments:
- decode_token_index: int32 [256, 4], P('replica'), may hold values from 0 to 76799
- token_embedding_table: bfloat16 [76800, 4096], P('replica', 'tp')
- input_norm_scale: bfloat16 [4096], P('tp'), may hold values from 0.099609375 to 1.8984375
- projection_weight: bfloat16 [2, 4096, 512], P(None, 'tp'), may hold values from -0.09375 to 0.09375
- input_factor: bfloat16 [2, 64, 4096], P(None, 'replica', 'tp'), may hold values from -0.09375 to 0.09375
- output_factor: bfloat16 [2, 512, 64], P(None, None, 'replica'), may hold values from -0.75 to 0.75
- cache: bfloat16 [2, 256, 2048, 512], P(None, 'replica', 'tp')
- cache_length_rows: int32 [256], P('replica'), may hold values from 2 to 2048, as said below
- queries: bfloat16 [256, 4, 4096], P('replica')
Outputs:
- attended: bfloat16 [256, 4, 4096], P('replica')
- new_kv: bfloat16 [2, 256, 4, 512], P(None, 'replica')
Inputs may be any that keep to these rules, and one draw needn't show every extreme that they name: `cache_length_rows`: every row has at least 2 cached positions; some row holds all 2048.
All inputs are finite; a program needn't handle non-finite values.
Results may differ from a plain program's by a relative error of at most 0.0066.
Values may be sent and summed in bfloat16 or wider, within the bound.
A program may use at most 64 MiB of HBM per device.

v0:
```python
import math

import jax
import jax.numpy as jnp
from jax import lax
from jax.sharding import PartitionSpec as P

KVH = 4
QH = 32
HD = 128


ROPE_THETA = 1000000.0
NEG = -1e30
EPS = 1e-06


def rotate(keys, positions):
    half = HD // 2
    index = jnp.arange(half, dtype=jnp.float32)
    freq = jnp.exp(index * (-2.0 * math.log(ROPE_THETA) / HD))
    angle = positions.astype(jnp.float32)[..., None] * freq
    cosine = jnp.cos(angle)[..., None, :]
    sine = jnp.sin(angle)[..., None, :]
    shaped = keys.reshape(keys.shape[:-1] + (KVH, HD))
    first = shaped[..., :half]
    second = shaped[..., half:]
    turned = jnp.concatenate(
        [first * cosine - second * sine, second * cosine + first * sine], axis=-1
    )
    return turned.reshape(keys.shape)


def finish(summed, positions):
    return jnp.stack([rotate(summed[0], positions), summed[1]]).astype(jnp.bfloat16)


def shards(
    decode_token_index,
    token_embedding_table,
    input_norm_scale,
    projection_weight,
    input_factor,
    output_factor,
    cache,
    cache_length_rows,
    queries,
):
    rows, steps = decode_token_index.shape
    voc_local, d_local = token_embedding_table.shape
    count_tok = rows * steps
    flat_ids = decode_token_index.reshape(count_tok)
    owner_start = lax.axis_index("replica") * voc_local
    every_id = lax.all_gather(flat_ids, "replica", axis=0, tiled=True)
    local = every_id - owner_start
    onehot = (local[:, None] == jnp.arange(voc_local, dtype=jnp.int32)[None, :]).astype(
        jnp.bfloat16
    )
    embedded = lax.psum_scatter(
        jnp.dot(onehot, token_embedding_table, preferred_element_type=jnp.float32),
        "replica",
        scatter_dimension=0,
        tiled=True,
    ).astype(jnp.bfloat16)
    wide = embedded.astype(jnp.float32)
    total_sq = lax.psum(jnp.sum(wide * wide, axis=1), "tp")
    d_model = d_local * lax.axis_size("tp")
    inverse = lax.rsqrt(total_sq / d_model + EPS)
    normed = (wide * input_norm_scale.astype(jnp.float32) * inverse[:, None]).astype(jnp.bfloat16)
    full_a, full_b = (
        lax.all_gather(input_factor, "replica", axis=1, tiled=True),
        lax.all_gather(output_factor, "replica", axis=2, tiled=True),
    )
    lowrank_update = jnp.einsum("amh,azm->ahz", full_a, full_b, preferred_element_type=jnp.float32)
    merged = (projection_weight.astype(jnp.float32) + lowrank_update).astype(jnp.bfloat16)
    partial_kv = jnp.einsum("nd,pdk->pnk", normed, merged, preferred_element_type=jnp.float32)
    positions = (cache_length_rows[:, None] + jnp.arange(steps, dtype=jnp.int32)[None, :]).reshape(
        count_tok
    )
    summed = lax.psum(partial_kv, "tp")
    fresh = finish(summed, positions)
    new_kv = fresh.reshape(2, rows, steps, fresh.shape[2])
    group = QH // KVH
    scale = 1.0 / math.sqrt(HD)
    c_loc = cache.shape[2]
    q_all = queries.reshape(rows, steps, KVH, group, HD)
    keys_local = cache[0].reshape(rows, c_loc, KVH, HD)
    values_local = cache[1].reshape(rows, c_loc, KVH, HD)
    fresh_k = new_kv[0].reshape(rows, steps, KVH, HD)
    fresh_v = new_kv[1].reshape(rows, steps, KVH, HD)
    old = (
        jnp.einsum("rtgjd,rpgd->rtgjp", q_all, keys_local, preferred_element_type=jnp.float32)
        * scale
    )
    new = (
        jnp.einsum("rtgjd,rsgd->rtgjs", q_all, fresh_k, preferred_element_type=jnp.float32) * scale
    )
    pos_local = lax.axis_index("tp") * c_loc + jnp.arange(c_loc, dtype=jnp.int32)
    valid = (pos_local[None, :] < cache_length_rows[:, None])[:, None, None, None, :]
    causal = (jnp.arange(steps)[:, None] >= jnp.arange(steps)[None, :])[None, :, None, None, :]
    old = jnp.where(valid, old, NEG)
    new = jnp.where(causal, new, NEG)
    local_top = jnp.maximum(jnp.max(old, axis=-1), jnp.max(new, axis=-1))
    top = lax.pmax(local_top, "tp")
    e_old = jnp.where(valid, jnp.exp(old - top[..., None]), 0.0)
    e_new = jnp.where(causal, jnp.exp(new - top[..., None]), 0.0)
    part_den = jnp.sum(e_old, axis=-1)
    part_num = jnp.einsum(
        "rtgjp,rpgd->rtgjd",
        e_old.astype(jnp.bfloat16),
        values_local,
        preferred_element_type=jnp.float32,
    )
    den, num = lax.psum((part_den, part_num), "tp")
    den = den + jnp.sum(e_new, axis=-1)
    num = num + jnp.einsum(
        "rtgjs,rsgd->rtgjd", e_new.astype(jnp.bfloat16), fresh_v, preferred_element_type=jnp.float32
    )
    attended = (num / den[..., None]).reshape(rows, steps, QH * HD).astype(jnp.bfloat16)
    return (attended, new_kv)


def solution(mesh):
    placed = (
        P("replica", None),
        P("replica", "tp"),
        P("tp"),
        P(None, "tp", None),
        P(None, "replica", "tp"),
        P(None, None, "replica"),
        P(None, "replica", "tp", None),
        P("replica"),
        P("replica", None, None),
    )
    return jax.shard_map(
        shards,
        mesh=mesh,
        in_specs=placed,
        out_specs=(P("replica", None, None), P(None, "replica", None, None)),
        check_vma=False,
    )
```

profile of v0, /device:TPU:1, one launch (start us, length us, event | category | flops | bytes accessed | tf_op | source)
XLA Modules:
  0.0 928.8 jit_solution(15736696809771956347)
XLA Ops:
  7.2 0.9 reshape.136
  8.1 1.3 dynamic-slice
  10.0 0.2 dynamic-update-slice
  10.3 29.3 %all-reduce = s32[1024]{0:T(1024)S(1)} all-reduce(s32[1024]{0:T(1024)S(1)} %dynamic-update-slice), channel_id=1, replica_groups=mesh['replica'=64,'tp'=8] {'replica'}, use_global_device_ids=true, to_apply=%add | all-reduce | flops 1024 | bytes 8192
  39.6 2.9 fusion
  42.6 0.6 copy-done.5
  43.3 0.1 copy-done.1
  43.4 0.2 reshape.134
  43.6 1.7 fusion.41
  45.3 1.3 copy.65
  46.6 0.5 copy.68
  47.2 154.8 %all_gather.9 = bf16[2,64,512]{2,0,1:T(2,128)(2,1)S(1)} all-gather(bf16[2,1,512]{2,0,1:T(2,128)(2,1)S(1)} %copy-done.2), channel_id=1, replica_groups=mesh['replica'=64,'tp'=8] {'replica'}, dimensions={1}, use_global_device_ids=true | all-gather | bytes 133120 | tf_op jit(solution)/shard_map/all_gather | solution.py:71
  202.0 146.5 %all_gather.10 = bf16[2,512,64]{1,0,2:T(2,128)(2,1)S(1)} all-gather(bf16[2,512,1]{1,0,2:T(2,128)(2,1)S(1)} %copy-done.3), channel_id=1, replica_groups=mesh['replica'=64,'tp'=8] {'replica'}, dimensions={2}, use_global_device_ids=true | all-gather | bytes 133120 | tf_op jit(solution)/shard_map/all_gather | solution.py:72
  348.6 0.1 multiply_cosine_fusion
  348.7 1.6 fusion.43
  350.3 246.8 %reduce-scatter.2.cloned.1.call-done = f32[16,512]{1,0:T(8,128)} async-done(((f32[1024,512]{1,0:T(8,128)}), f32[16,512]{1,0:T(8,128)}) %reduce-scatter.2.cloned.1.call-update) | async-done | bytes 32784 | tf_op jit(solution)/shard_map/reduce_scatter | solution.py:59
  597.1 0.9 fusion.31
  598.0 29.6 %psum.28 = f32[16]{0:T(128)S(1)} all-reduce(f32[16]{0:T(128)S(1)} %fusion.31), channel_id=1, replica_groups=mesh['replica'=64,'tp'=8] {'tp'}, use_global_device_ids=true, to_apply=%region_3.0 | all-reduce | flops 16 | bytes 128 | tf_op jit(solution)/shard_map/psum | solution.py:66
  627.6 2.5 fusion.10
  630.2 115.2 %all-reduce.4.cloned.1.call-done = f32[2,16,512]{2,1,0:T(8,128)} async-done(((f32[2,16,512]{2,1,0:T(8,128)}), f32[2,16,512]{2,1,0:T(8,128)}) %all-reduce.4.cloned.1.call-update) | async-done | bytes 65552 | tf_op jit(solution)/shard_map/psum | solution.py:80
  745.4 0.8 slice.31
  746.4 0.7 fusion.44
  747.1 43.0 %pmax.7 = f32[4,4,4,8]{3,1,2,0:T(4,128)S(1)} all-reduce(f32[4,4,4,8]{3,1,2,0:T(4,128)S(1)} %max.5), channel_id=1, replica_groups=mesh['replica'=64,'tp'=8] {'tp'}, use_global_device_ids=true, to_apply=%region_6.7 | all-reduce | flops 512 | bytes 4096 | tf_op jit(solution)/shard_map/pmax | solution.py:104
  790.1 1.2 convolution_bitcast_fusion
  791.3 0.3 fusion.11
  791.6 0.8 slice.37
  792.4 42.0 %psum.31 = f32[4,4,4,8]{3,1,2,0:T(4,128)S(1)} all-reduce(f32[4,4,4,8]{3,1,2,0:T(4,128)S(1)} %fusion.11), channel_id=1, replica_groups=mesh['replica'=64,'tp'=8] {'tp'}, use_global_device_ids=true, to_apply=%region_9.10 | all-reduce | flops 512 | bytes 4096 | tf_op jit(solution)/shard_map/psum | solution.py:114
  834.4 0.2 fusion.23
  834.6 0.6 pad_maximum_fusion
  835.2 85.1 %all-reduce.6.cloned.1.call-done = f32[4,4,4,8,128]{4,3,1,2,0:T(8,128)} async-done(((f32[4,4,4,8,128]{4,3,1,2,0:T(8,128)}), f32[4,4,4,8,128]{4,3,1,2,0:T(8,128)}) %all-reduce.6.cloned.1.call-update) | async-done | bytes 262160 | tf_op jit(solution)/shard_map/psum | solution.py:114
  920.3 1.3 fusion.7
  921.6 0.7 convert_element_type.54
  (37 shorter events, 0.8 us)
Async XLA Ops:
  7.2 32.4 %copy-start = (bf16[1200,512]{1,0:T(8,128)(2,1)S(1)}, bf16[1200,512]{1,0:T(8,128)(2,1)}, u32[]{:S(2)}) copy-start(bf16[1200,512]{1,0:T(8,128)(2,1)} %param.10) | copy-start | bytes 3686404
  7.2 589.9 %reduce-scatter.2.cloned.1.call-start = ((), (), s32[]{:S(2)}) async-start(), calls=%async_computation.1 | async-start | bytes 2129920 | tf_op jit(solution)/shard_map/reduce_scatter | solution.py:59
  42.5 0.7 copy-start.5
  42.5 0.7 copy-start.4
  42.5 0.9 copy-start.1
  42.5 702.9 %all-reduce.4.cloned.1.call-start = ((), (), s32[]{:S(2)}) async-start(), calls=%async_computation.2 | async-start | bytes 131072 | tf_op jit(solution)/shard_map/psum | solution.py:80
  45.3 1.9 copy-start.2
  45.3 156.7 %copy-start.3 = (bf16[2,512,1]{1,0,2:T(2,128)(2,1)S(1)}, bf16[2,512,1]{1,0,2:T(2,128)(2,1)}, u32[]{:S(2)}) copy-start(bf16[2,512,1]{1,0,2:T(2,128)(2,1)} %param.14) | copy-start | bytes 6148
  630.1 290.2 %all-reduce.6.cloned.1.call-start = ((), (), s32[]{:S(2)}) async-start(), calls=%async_computation.3 | async-start | bytes 524288 | tf_op jit(solution)/shard_map/psum | solution.py:114
Sparse Core Ops, SparseCore 0:
  42.6 554.4 reduce-scatter.1
  630.2 115.1 all-reduce.3
  791.4 128.8 all-reduce.5
where the time goes:
time: 934 us; the launch traced here: 929 us
  waiting for transfers between devices  447 us (48%)
  blocking collectives  445 us (48%)
  between operations  14.6 us (2%)
  matrix products  10.1 us (1%)
    reduce_scatter x1, waiting for transfers between devices, shards(): lax.psum_scatter(jnp.dot(onehot, token_embedding_table, preferred_element...  247 us
    all_gather x1, blocking collectives, shards(): lax.all_gather(input_factor, 'replica', axis=1, tiled=True)  155 us
    all_gather x1, blocking collectives, shards(): lax.all_gather(output_factor, 'replica', axis=2, tiled=True)  146 us
    psum x1, waiting for transfers between devices, shards(): summed = lax.psum(partial_kv, 'tp')  115 us
    psum x1, waiting for transfers between devices, shards(): den, num = lax.psum((part_den, part_num), 'tp')  85.1 us
    pmax x1, blocking collectives, shards(): top = lax.pmax(local_top, 'tp')  43 us
    psum x1, blocking collectives, shards(): den, num = lax.psum((part_den, part_num), 'tp')  42 us
    psum x1, blocking collectives, shards(): total_sq = lax.psum(jnp.sum(wide * wide, axis=1), 'tp')  29.6 us
  transfers between devices with their start and end apart: 3, of which 3 were waited for; matrix products, arithmetic and copies ran while one was open for 1% of the time, Pallas kernels for 0%

commit v1 on v0

v1 whole, which is shorter than its diff:
```python
import functools
import math

import jax
import jax.numpy as jnp
from jax import lax
from jax.experimental import pallas as pl
from jax.experimental.pallas import tpu as pltpu
from jax.sharding import PartitionSpec as P

X, ZH, Y, C = 4, 2, 4, 2
T = 8
GROUP = ZH * Y * C
KVH = 4
QH = 32
HD = 128
ROPE_THETA = 1000000.0
NEG = -1e30
EPS = 1e-06
SHRINK = 2.0**-20
LANES = 128
MESH = pl.DeviceIdType.MESH
F32 = jnp.float32
BF16 = jnp.bfloat16


def iota(shape, dim):
    return lax.broadcasted_iota(jnp.int32, shape, dim)


def nt(a, b):
    return lax.dot_general(a, b, (((1,), (1,)), ((), ())), preferred_element_type=F32)


def tn(a, b):
    return lax.dot_general(a, b, (((0,), (0,)), ((), ())), preferred_element_type=F32)


def loop(lo, hi, fn):
    def step(i, carry):
        fn(i)
        return carry

    lax.fori_loop(lo, hi, step, 0)


def kernel(
    ids_ref, len_ref, gain_ref, a_ref, b_ref, table_hbm, w_hbm, cache_hbm, q_hbm,
    att_ref, kv_ref,
    table, weight, cache, q_in, load_sem,
    ids_one, ids_all, fac_one, fac_all, qs, qbd,
    core_out, core_in, plane_out, plane_in, merged,
    part_out, part_in, stat_out, stat_in, old_all, old_stat,
    kv_out, kv_in, sq_out, sq_in, kv_all,
    id1_s, id1_r, id2_s, id2_r, fa1_s, fa1_r, fa2_s, fa2_r,
    core_s, core_r, plane_s, plane_r, part_s, part_r, stat_s, stat_r,
    old_s, old_r, olst_s, olst_r, kv_s, kv_r, sq_s, sq_r, new_s, new_r,
):
    r = lax.axis_index("replica")
    t = lax.axis_index("tp")
    x = r // GROUP
    m = r % GROUP
    zh = m // (Y * C)
    y = (m // C) % Y
    c = m % C
    rows, steps = ids_ref.shape
    toks = rows * steps
    voc, feat = table.shape
    c_loc = cache.shape[2]
    features = feat * T
    my_row = t // 2
    pair = t % 2

    def rep(x_, zh_, y_, c_):
        return ((x_ * ZH + zh_) * Y + y_) * C + c_

    def remote(src, dst, send, recv, where):
        return pltpu.make_async_remote_copy(
            src_ref=src, dst_ref=dst, send_sem=send, recv_sem=recv,
            device_id=where, device_id_type=MESH,
        )

    loads = [
        pltpu.make_async_copy(q_hbm, q_in, load_sem.at[0]),
        pltpu.make_async_copy(cache_hbm, cache, load_sem.at[1]),
        pltpu.make_async_copy(table_hbm, table, load_sem.at[2]),
        pltpu.make_async_copy(w_hbm, weight, load_sem.at[3]),
    ]
    for load in loads:
        load.start()

    barrier = pltpu.get_barrier_semaphore()

    def hello(where):
        pl.semaphore_signal(barrier, inc=1, device_id=where, device_id_type=MESH)

    loop(1, GROUP, lambda d: hello((x * GROUP + (m + d) % GROUP, t)))
    loop(Y, X * Y, lambda d: hello((rep((x + d // Y) % X, zh, (y + d % Y) % Y, c), t)))
    loop(ZH, ZH * T, lambda d: hello((rep(x, (zh + d % ZH) % ZH, y, c), (t + d // ZH) % T)))

    lane = iota((1, LANES), 1)
    row = jnp.zeros((1, LANES), jnp.int32)
    base = (y * ZH + zh) * toks
    for k in range(toks):
        row = jnp.where(lane == base + k, ids_ref[k // steps, k % steps], row)
    ids_one[m] = row
    chunks = feat // LANES
    pieces = []
    for ref in (a_ref, b_ref):
        for p in range(2):
            for i in range(chunks):
                pieces.append(ref[p : p + 1, i * LANES : (i + 1) * LANES].astype(F32))
    fac_one[m] = jnp.concatenate(pieces, axis=0).astype(BF16)

    pl.semaphore_wait(barrier, (GROUP - 1) + (X - 1) * Y + (T - 1) * ZH)

    def id1(d):
        other = (m + d) % GROUP
        return remote(ids_one.at[m], ids_one.at[m], id1_s.at[d], id1_r.at[m], (x * GROUP + other, t))

    def id1_in(d):
        other = (m + d) % GROUP
        return remote(ids_one.at[m], ids_one.at[other], id1_s.at[d], id1_r.at[other], (x * GROUP + other, t))

    def fa1(d):
        other = (m + d) % GROUP
        return remote(fac_one.at[m], fac_one.at[m], fa1_s.at[d], fa1_r.at[m], (x * GROUP + other, t))

    def fa1_in(d):
        other = (m + d) % GROUP
        return remote(fac_one.at[m], fac_one.at[other], fa1_s.at[d], fa1_r.at[other], (x * GROUP + other, t))

    loop(1, GROUP, lambda d: id1(d).start())
    loop(1, GROUP, lambda d: fa1(d).start())

    loads[0].wait()
    qbd[...] = jnp.zeros_like(qbd)
    for a in range(rows):
        q32 = q_in[a].astype(F32)
        tall = jnp.concatenate([q32[:, h * HD : (h + 1) * HD] for h in range(QH)], axis=0).astype(BF16)
        qs[a] = tall
        span = tall.shape[0] // KVH
        for g in range(KVH):
            qbd[a, g * span : (g + 1) * span, g * HD : (g + 1) * HD] = tall[g * span : (g + 1) * span, :]
    loads[1].wait()
    scale = 1.0 / math.sqrt(HD)

    def attend(a):
        s = nt(cache[0, a], qbd[a]) * scale
        valid = t * c_loc + iota(s.shape, 0) < len_ref[a]
        s = jnp.where(valid, s, NEG)
        top = jnp.max(s, axis=0, keepdims=True)
        e = jnp.where(valid, jnp.exp(s - top), 0.0)
        den = jnp.sum(e, axis=0, keepdims=True)
        num = tn(e.astype(BF16), cache[1, a])
        span = num.shape[0] // KVH
        half = 2 * span
        for g in range(KVH):
            part_out[2 * a + g // 2, (g % 2) * span : (g % 2 + 1) * span, :] = num[
                g * span : (g + 1) * span, g * HD : (g + 1) * HD
            ].astype(BF16)
        stat_out[a] = jnp.concatenate([top, den], axis=0)

    def part(d):
        to = (t + d) % T
        return remote(part_out.at[to], part_in.at[t], part_s.at[d], part_r.at[t], (r, to))

    def part_wait(d):
        to = (t + d) % T
        return remote(part_out.at[to], part_in.at[to], part_s.at[d], part_r.at[to], (r, to))

    def stat(d):
        to = (t + d) % T
        return remote(stat_out.at[to // 2], stat_in.at[t], stat_s.at[d], stat_r.at[t], (r, to))

    def stat_wait(d):
        to = (t + d) % T
        return remote(stat_out.at[to // 2], stat_in.at[to], stat_s.at[d], stat_r.at[to], (r, to))

    loop(0, rows // 2, attend)

    loop(1, GROUP, lambda d: id1_in(d).wait_recv())
    gathered = []
    for c_ in range(C):
        total = ids_one[c_]
        for i in range(1, ZH * Y):
            total = total + ids_one[i * C + c_]
        gathered.append(total)
    ids_all[x] = jnp.concatenate(gathered, axis=0)

    def id2(d):
        return remote(ids_all.at[x], ids_all.at[x], id2_s.at[d], id2_r.at[x], (rep((x + d) % X, zh, y, c), t))

    def id2_in(d):
        other = (x + d) % X
        return remote(ids_all.at[x], ids_all.at[other], id2_s.at[d], id2_r.at[other], (rep(other, zh, y, c), t))

    loop(1, X, lambda d: id2(d).start())

    loop(1, GROUP, lambda d: fa1_in(d).wait_recv())
    size = GROUP * GROUP
    flat = fac_one[...].reshape(GROUP * 16, LANES)
    o, i = iota((16 * GROUP, 16 * GROUP), 0), iota((16 * GROUP, 16 * GROUP), 1)
    perm = ((o // GROUP == i % 16) & (o % GROUP == i // 16)).astype(F32).astype(BF16)
    fac_all[x] = jnp.dot(perm, flat, preferred_element_type=F32).astype(BF16).reshape(16, GROUP, LANES)

    def fa2(d):
        return remote(fac_all.at[x], fac_all.at[x], fa2_s.at[d], fa2_r.at[x], (rep((x + d) % X, zh, y, c), t))

    def fa2_in(d):
        other = (x + d) % X
        return remote(fac_all.at[x], fac_all.at[other], fa2_s.at[d], fa2_r.at[other], (rep(other, zh, y, c), t))

    loop(1, X, lambda d: fa2(d).start())

    loop(rows // 2, rows, attend)
    loop(1, T, lambda d: stat(d).start())
    loop(1, T, lambda d: part(d).start())

    loop(1, X, lambda d: id2_in(d).wait_recv())
    loads[2].wait()
    start = r * voc

    def lookup(x_, c_):
        wide = jnp.broadcast_to(ids_all[x_, pl.ds(c_, 1), :], (LANES, LANES))
        ids = jnp.transpose(wide)[:, 0:1] - start
        onehot = (ids == iota((LANES, voc), 1)).astype(F32).astype(BF16)
        return jnp.dot(onehot, table[...], preferred_element_type=F32)

    share = ZH * toks

    def core(k):
        return remote(core_out.at[k], core_in.at[k], core_s.at[k], core_r.at[k], (rep(x, zh, y, 1 - c), t))

    def first(k):
        core_out[k] = lookup((x + 1 + k) % X, 1 - c).astype(BF16)
        core(k).start()

    loop(0, X, first)

    def plane(d):
        dx, dy = d // Y, d % Y
        x_, y_ = (x + dx) % X, (y + dy) % Y
        return remote(
            plane_out.at[dx, y_], plane_in.at[x * Y + y], plane_s.at[d], plane_r.at[x * Y + y],
            (rep(x_, zh, y_, c), t),
        )

    def plane_wait(d):
        x_, y_ = (x + d // Y) % X, (y + d % Y) % Y
        slot = x_ * Y + y_
        return remote(
            plane_out.at[d // Y, y_], plane_in.at[slot], plane_s.at[d], plane_r.at[slot],
            (rep(x_, zh, y_, c), t),
        )

    def second(k):
        dx = (1 + k) % X
        found = lookup((x + dx) % X, c)
        core(k).wait_recv()
        plane_out[dx] = (found + core_in[k].astype(F32)).astype(BF16).reshape(Y, share, feat)

    def second_far(k):
        second(k)
        loop(0, Y, lambda dy: plane((1 + k) * Y + dy).start())

    loop(0, X - 1, second_far)
    second(X - 1)
    loop(1, Y, lambda dy: plane(dy).start())

    loop(1, X, lambda d: fa2_in(d).wait_recv())
    loads[3].wait()
    for p in range(2):
        full = []
        for side in range(2):
            full.append(
                jnp.concatenate(
                    [
                        fac_all[:, (side * 2 + p) * chunks + i].reshape(X * GROUP, LANES)
                        for i in range(chunks)
                    ],
                    axis=1,
                )
            )
        update = tn(full[0], full[1])
        merged[p] = (weight[p].astype(F32) + update).astype(BF16)

    loop(1, T, lambda d: stat_wait(d).wait_recv())
    stat_in[t] = stat_out[my_row]
    tops = jnp.concatenate([stat_in[i][0:1] for i in range(T)], axis=0)
    dens = jnp.concatenate([stat_in[i][1:2] for i in range(T)], axis=0)
    top = jnp.max(tops, axis=0, keepdims=True)
    w = jnp.exp(tops - top)
    den = jnp.sum(dens * w, axis=0, keepdims=True)
    old_stat[t] = jnp.concatenate([top, den], axis=0)
    w = jnp.transpose(jnp.concatenate([w / den, jnp.zeros((LANES - T, LANES), F32)], axis=0))
    w = jnp.where(pair == 0, w[: LANES // 2], w[LANES // 2 :])
    loop(1, T, lambda d: part_wait(d).wait_recv())
    part_in[t] = part_out[t]
    mix = part_in[0].astype(F32) * w[:, 0:1]
    for i in range(1, T):
        mix = mix + part_in[i].astype(F32) * w[:, i : i + 1]
    old_all[t] = mix.astype(BF16)

    def old(d):
        to = (t + d) % T
        return remote(old_all.at[t], old_all.at[t], old_s.at[d], old_r.at[t], (r, to))

    def old_wait(d):
        to = (t + d) % T
        return remote(old_all.at[t], old_all.at[to], old_s.at[d], old_r.at[to], (r, to))

    def olst(d):
        to = (t + d) % T
        return remote(old_stat.at[t], old_stat.at[t], olst_s.at[d], olst_r.at[t], (r, to))

    def olst_wait(d):
        to = (t + d) % T
        return remote(old_stat.at[t], old_stat.at[to], olst_s.at[d], olst_r.at[to], (r, to))

    loop(1, T, lambda d: olst(d).start())
    loop(1, T, lambda d: old(d).start())

    half = HD // 2
    keyed = 2 * steps
    position = (len_ref[my_row] + iota((keyed, HD), 0) % steps).astype(F32)
    column = iota((keyed, HD), 1)
    freq = jnp.exp((column % half).astype(F32) * (-2.0 * math.log(ROPE_THETA) / HD))
    angle = position * freq
    cosine = jnp.cos(angle)
    sine = jnp.where(column < half, -jnp.sin(angle), jnp.sin(angle))

    loop(1, X * Y, lambda d: plane_wait(d).wait_recv())
    plane_in[x * Y + y] = plane_out[0, y]
    embedded = plane_in[0].astype(F32)
    for i in range(1, X * Y):
        embedded = embedded + plane_in[i].astype(F32)
    squares = jnp.sum(embedded * embedded, axis=1, keepdims=True)
    squares = jnp.where(iota((share, LANES), 0) == iota((share, LANES), 1), squares, 0.0)
    sq_out[...] = jnp.sum(squares, axis=0, keepdims=True)
    ready = (embedded * (gain_ref[...].astype(F32) * SHRINK)).astype(BF16)
    proj = [jnp.dot(ready, merged[p], preferred_element_type=F32) for p in range(2)]
    for zh_ in range(ZH):
        for t_ in range(T):
            at = zh_ * toks + (t_ // 2) * steps
            cols = (t_ % 2) * 2 * HD
            kv_out[zh_, t_] = jnp.concatenate(
                [
                    proj[p][at : at + steps, cols + i * HD : cols + (i + 1) * HD]
                    for p in range(2)
                    for i in range(2)
                ],
                axis=0,
            ).astype(BF16)

    def ring(d):
        return (zh + d // T) % ZH, (t + d % T) % T

    def kv(d):
        zh_, t_ = ring(d)
        me = zh * T + t
        return remote(kv_out.at[zh_, t_], kv_in.at[me], kv_s.at[d], kv_r.at[me], (rep(x, zh_, y, c), t_))

    def kv_wait(d):
        zh_, t_ = ring(d)
        slot = zh_ * T + t_
        return remote(kv_out.at[zh_, t_], kv_in.at[slot], kv_s.at[d], kv_r.at[slot], (rep(x, zh_, y, c), t_))

    def sq(d):
        zh_, t_ = ring(d)
        me = zh * T + t
        return remote(sq_out, sq_in.at[me], sq_s.at[d], sq_r.at[me], (rep(x, zh_, y, c), t_))

    def sq_wait(d):
        zh_, t_ = ring(d)
        slot = zh_ * T + t_
        return remote(sq_out, sq_in.at[slot], sq_s.at[d], sq_r.at[slot], (rep(x, zh_, y, c), t_))

    loop(1, ZH * T, lambda d: sq(d).start())
    loop(1, ZH * T, lambda d: kv(d).start())
    kv_in[zh * T + t] = kv_out[zh, t]
    sq_in[zh * T + t] = sq_out[...]

    loop(1, ZH * T, lambda d: sq_wait(d).wait_recv())
    sq_sum = sq_in[0]
    for i in range(1, ZH * T):
        sq_sum = sq_sum + sq_in[i]
    inverse = lax.rsqrt(sq_sum / features + EPS) * (1.0 / SHRINK)
    keep = iota((4 * steps, LANES), 1) == zh * toks + my_row * steps + iota((4 * steps, LANES), 0) % steps
    factor = jnp.sum(jnp.where(keep, inverse, 0.0), axis=1, keepdims=True)
    loop(1, ZH * T, lambda d: kv_wait(d).wait_recv())
    fresh = kv_in[0].astype(F32)
    for i in range(1, ZH * T):
        fresh = fresh + kv_in[i].astype(F32)
    fresh = fresh * factor
    keys = fresh[:keyed]
    keys = keys * cosine + pltpu.roll(keys, half, 1) * sine
    kv_all[t] = jnp.concatenate([keys, fresh[keyed:]], axis=0).astype(BF16)

    def new(d):
        to = (t + d) % T
        return remote(kv_all.at[t], kv_all.at[t], new_s.at[d], new_r.at[t], (r, to))

    def new_wait(d):
        to = (t + d) % T
        return remote(kv_all.at[t], kv_all.at[to], new_s.at[d], new_r.at[to], (r, to))

    loop(1, T, lambda d: new(d).start())

    loop(1, T, lambda d: olst_wait(d).wait_recv())
    loop(1, T, lambda d: old_wait(d).wait_recv())
    loop(1, T, lambda d: new_wait(d).wait_recv())
    at_lane = iota((keyed, LANES), 1)
    at_row = iota((keyed, LANES), 0)
    span = LANES // KVH
    causal = (at_row // steps == (at_lane // span) % 2) & (at_row % steps <= at_lane % steps)
    low = lane < LANES // 2
    shares, news = [], []
    for a in range(rows):
        s = jnp.where(
            at_lane < LANES // 2, nt(kv_all[2 * a], qs[a])[:keyed], nt(kv_all[2 * a + 1], qs[a])[:keyed]
        ) * scale
        s = jnp.where(causal, s, NEG)
        stats = jnp.where(low, old_stat[2 * a], old_stat[2 * a + 1])
        old_top, old_den = stats[0:1], stats[1:2]
        top = jnp.maximum(old_top, jnp.max(s, axis=0, keepdims=True))
        e = jnp.where(causal, jnp.exp(s - top), 0.0)
        old_den = old_den * jnp.exp(old_top - top)
        den = old_den + jnp.sum(e, axis=0, keepdims=True)
        shares.append(old_den / den)
        news.append(e / den)
    cols = jnp.transpose(jnp.concatenate(shares + [jnp.zeros((LANES - rows, LANES), F32)], axis=0))
    for a in range(rows):
        e = jnp.concatenate([jnp.zeros_like(news[a]), news[a]], axis=0).astype(BF16)
        lower = tn(e, kv_all[2 * a])[: LANES // 2]
        upper = tn(e, kv_all[2 * a + 1])[LANES // 2 :]
        add = jnp.concatenate([lower, upper], axis=0)
        oldies = jnp.concatenate([old_all[2 * a], old_all[2 * a + 1]], axis=0).astype(F32)
        out = oldies * cols[:, a : a + 1] + add
        for h in range(QH):
            att_ref[a, :, h * HD : (h + 1) * HD] = out[h * steps : (h + 1) * steps].astype(BF16)
        for g in range(KVH):
            got = kv_all[2 * a + g // 2].astype(F32)
            for p in range(2):
                at = (p * 2 + g % 2) * steps
                kv_ref[p, a, :, g * HD : (g + 1) * HD] = got[at : at + steps].astype(BF16)

    loop(1, GROUP, lambda d: id1(d).wait_send())
    loop(1, GROUP, lambda d: fa1(d).wait_send())
    loop(1, X, lambda d: id2(d).wait_send())
    loop(1, X, lambda d: fa2(d).wait_send())
    loop(0, X, lambda d: core(d).wait_send())
    loop(1, X * Y, lambda d: plane(d).wait_send())
    loop(1, T, lambda d: stat(d).wait_send())
    loop(1, T, lambda d: part(d).wait_send())
    loop(1, T, lambda d: olst(d).wait_send())
    loop(1, T, lambda d: old(d).wait_send())
    loop(1, ZH * T, lambda d: sq(d).wait_send())
    loop(1, ZH * T, lambda d: kv(d).wait_send())
    loop(1, T, lambda d: new(d).wait_send())


def shards(ids, table, gain, weight, in_factor, out_factor, cache, lengths, queries):
    rows, steps = ids.shape
    voc, feat = table.shape
    vmem = pl.BlockSpec(memory_space=pltpu.VMEM)
    smem = pl.BlockSpec(memory_space=pltpu.SMEM)
    hbm = pl.BlockSpec(memory_space=pl.ANY)
    share = ZH * rows * steps
    dma = pltpu.SemaphoreType.DMA
    half = LANES // 2
    scratch = [
        pltpu.VMEM(table.shape, BF16),
        pltpu.VMEM(weight.shape, BF16),
        pltpu.VMEM(cache.shape, BF16),
        pltpu.VMEM(queries.shape, BF16),
        dma((4,)),
        pltpu.VMEM((GROUP, 1, LANES), jnp.int32),
        pltpu.VMEM((X, C, LANES), jnp.int32),
        pltpu.VMEM((GROUP, 16, LANES), BF16),
        pltpu.VMEM((X, 16, GROUP, LANES), BF16),
        pltpu.VMEM((rows, LANES, HD), BF16),
        pltpu.VMEM((rows, LANES, KVH * HD), BF16),
        pltpu.VMEM((X, LANES, feat), BF16),
        pltpu.VMEM((X, LANES, feat), BF16),
        pltpu.VMEM((X, Y, share, feat), BF16),
        pltpu.VMEM((X * Y, share, feat), BF16),
        pltpu.VMEM(weight.shape, BF16),
        pltpu.VMEM((T, half, HD), BF16),
        pltpu.VMEM((T, half, HD), BF16),
        pltpu.VMEM((rows, 2, LANES), F32),
        pltpu.VMEM((T, 2, LANES), F32),
        pltpu.VMEM((T, half, HD), BF16),
        pltpu.VMEM((T, 2, LANES), F32),
        pltpu.VMEM((ZH, T, 4 * steps, HD), BF16),
        pltpu.VMEM((ZH * T, 4 * steps, HD), BF16),
        pltpu.VMEM((1, LANES), F32),
        pltpu.VMEM((ZH * T, 1, LANES), F32),
        pltpu.VMEM((T, 4 * steps, HD), BF16),
    ]
    for count in (GROUP, GROUP, X, X, GROUP, GROUP, X, X, X, X, X * Y, X * Y, T, T, T, T):
        scratch.append(dma((count,)))
    for count in (T, T, T, T, ZH * T, ZH * T, ZH * T, ZH * T, T, T):
        scratch.append(dma((count,)))
    return pl.pallas_call(
        kernel,
        out_shape=(
            jax.ShapeDtypeStruct((rows, steps, QH * HD), BF16),
            jax.ShapeDtypeStruct((2, rows, steps, KVH * HD), BF16),
        ),
        in_specs=[smem, smem, vmem, vmem, vmem, hbm, hbm, hbm, hbm],
        out_specs=(vmem, vmem),
        scratch_shapes=scratch,
        compiler_params=pltpu.CompilerParams(
            collective_id=0, has_side_effects=True, vmem_limit_bytes=48 * 1024 * 1024
        ),
        cost_estimate=pl.CostEstimate(flops=2_000_000_000, bytes_accessed=5_000_000, transcendentals=200_000),
    )(
        ids,
        lengths,
        gain.reshape(1, feat),
        in_factor.reshape(2, feat),
        out_factor.reshape(2, feat),
        table,
        weight,
        cache,
        queries,
    )


def solution(mesh):
    placed = (
        P("replica", None),
        P("replica", "tp"),
        P("tp"),
        P(None, "tp", None),
        P(None, "replica", "tp"),
        P(None, None, "replica"),
        P(None, "replica", "tp", None),
        P("replica"),
        P("replica", None, None),
    )
    return jax.shard_map(
        shards,
        mesh=mesh,
        in_specs=placed,
        out_specs=(P("replica", None, None), P(None, "replica", None, None)),
        check_vma=False,
    )
```

time: 934 us -> 71.6 us (0.08)
  waiting for transfers between devices: 447 us -> 0 us
  blocking collectives: 445 us -> 0 us
  Pallas kernels: 0 us -> 60.9 us
  between operations: 14.6 us -> 0.65 us
  matrix products: 10.1 us -> 0 us
    all_gather x2 -> x0, blocking collectives: 301 us -> none  [the longest x1 155 us: shards(): lax.all_gather(input_factor, 'replica', axis=1, tiled=True)]
    reduce_scatter x1 -> x0, waiting for transfers between devices: 247 us -> none  [shards(): lax.psum_scatter(jnp.dot(onehot, token_embedding_table, preferred_element...]
    psum x2 -> x0, waiting for transfers between devices: 200 us -> none  [the longest x1 115 us: shards(): summed = lax.psum(partial_kv, 'tp')]
    psum x2 -> x0, blocking collectives: 71.6 us -> none  [the longest x1 42 us: shards(): den, num = lax.psum((part_den, part_num), 'tp')]
    pallas_call x0 -> x1, Pallas kernels: none -> 60.9 us  [shards(): pl.pallas_call(kernel, out_shape=(jax.ShapeDtypeStruct((rows, steps, QH *...]
    pmax x1 -> x0, blocking collectives: 43 us -> none  [shards(): top = lax.pmax(local_top, 'tp')]
    unnamed x1 -> x0, blocking collectives: 29.3 us -> none
    dot_general x6 -> x0, matrix products: 10.1 us -> none  [the longest x1 2.92 us: shards(): jnp.dot(onehot, token_embedding_table, preferred_element_type=jnp.float32)]
  transfers between devices with their start and end apart: 3 -> 0, of which waited for: 3 -> 0; matrix products, arithmetic and copies ran while one was open for 1% -> 0% of each run, Pallas kernels for 0% -> 0%
where the time goes in v1:
time: 71.6 us; the launch traced here: 71.2 us
  Pallas kernels  60.9 us (85%)
  local copies, waits for them, and re-layouts  9.66 us (13%)
    pallas_call x1, Pallas kernels, shards(): pl.pallas_call(kernel, out_shape=(jax.ShapeDtypeStruct((rows, steps, QH *...  60.9 us
    unnamed x18, local copies, waits for them, and re-layouts  8.98 us

profile of v1, /device:TPU:1, one launch (start us, length us, event | category | flops | bytes accessed | tf_op | source)
XLA Modules:
  0.0 71.2 jit_solution(18192513419285584853)
XLA Ops:
  0.6 0.7 reshape.13.gain_ref
  1.3 0.0 copy-start
  1.3 1.6 %copy-done = bf16[2,4,256,512]{3,2,1,0:T(8,128)(2,1)S(1)} copy-done((bf16[2,4,256,512]{3,2,1,0:T(8,128)(2,1)S(1)}, bf16[2,4,256,512]{3,2,1,0:T(8,128)(2,1)}, u32[]{:S(2)}) %copy-start) | copy-done | bytes 2097176
  2.9 0.0 copy-start.1
  2.9 1.3 %copy-done.1 = bf16[1200,512]{1,0:T(8,128)(2,1)S(1)} copy-done((bf16[1200,512]{1,0:T(8,128)(2,1)S(1)}, bf16[1200,512]{1,0:T(8,128)(2,1)}, u32[]{:S(2)}) %copy-start.1) | copy-done | bytes 1228824
  4.2 0.0 copy-start.2
  4.2 1.2 %copy-done.2 = bf16[2,512,512]{2,1,0:T(8,128)(2,1)S(1)} copy-done((bf16[2,512,512]{2,1,0:T(8,128)(2,1)S(1)}, bf16[2,512,512]{2,1,0:T(8,128)(2,1)}, u32[]{:S(2)}) %copy-start.2) | copy-done | bytes 1048600
  5.4 0.0 copy-start.3
  5.4 0.9 %copy-done.3 = bf16[4,4,4096]{2,1,0:T(4,128)(2,1)S(1)} copy-done((bf16[4,4,4096]{2,1,0:T(4,128)(2,1)S(1)}, bf16[4,4,4096]{2,1,0:T(4,128)(2,1)}, u32[]{:S(2)}) %copy-start.3) | copy-done | bytes 131096
  6.3 0.0 copy-start.4
  6.3 0.7 copy-done.4
  7.0 0.0 copy-start.5
  7.0 0.7 copy-done.5
  7.7 0.0 copy-start.6
  7.7 0.7 copy-done.6
  8.4 0.0 copy-start.7
  8.4 0.7 copy-done.7
  9.0 60.9 %shard_map.104 = (bf16[4,4,4096]{2,1,0:T(4,128)(2,1)S(1)}, bf16[2,4,4,512]{3,2,1,0:T(4,128)(2,1)S(1)}) custom-call(s32[4,4]{1,0:T(4,128)S(1)} %copy-done.4, s32[4]{0:T(128)S(1)} %copy-done.7, bf16[1,512]{1,0:T(2,128)(2,1)S(1)} %reshape.13.gain_ref, bf16[2,512]{1,0:T(2,128)(2,1)S(1)} %bitcast.2, bf16[2,512]{1,0:T(2,128)(2,1)S(1)} %bitcast.3, ...), custom_call_target="tpu_custom_call" | custom-call | flops 2000000000 | bytes 5000000 | tf_op jit(solution)/shard_map/pallas_call | solution.py:505
  70.0 0.7 copy.13
  70.6 0.6 copy.14
Async XLA Ops:
  1.3 1.6 %copy-start = (bf16[2,4,256,512]{3,2,1,0:T(8,128)(2,1)S(1)}, bf16[2,4,256,512]{3,2,1,0:T(8,128)(2,1)}, u32[]{:S(2)}) copy-start(bf16[2,4,256,512]{3,2,1,0:T(8,128)(2,1)} %cache_hbm.1) | copy-start | bytes 6291460
  2.9 1.3 %copy-start.1 = (bf16[1200,512]{1,0:T(8,128)(2,1)S(1)}, bf16[1200,512]{1,0:T(8,128)(2,1)}, u32[]{:S(2)}) copy-start(bf16[1200,512]{1,0:T(8,128)(2,1)} %table_hbm.1) | copy-start | bytes 3686404
  4.2 1.2 %copy-start.2 = (bf16[2,512,512]{2,1,0:T(8,128)(2,1)S(1)}, bf16[2,512,512]{2,1,0:T(8,128)(2,1)}, u32[]{:S(2)}) copy-start(bf16[2,512,512]{2,1,0:T(8,128)(2,1)} %w_hbm.1) | copy-start | bytes 3145732
  5.4 0.9 %copy-start.3 = (bf16[4,4,4096]{2,1,0:T(4,128)(2,1)S(1)}, bf16[4,4,4096]{2,1,0:T(4,128)(2,1)}, u32[]{:S(2)}) copy-start(bf16[4,4,4096]{2,1,0:T(4,128)(2,1)} %q_hbm.1) | copy-start | bytes 393220
  6.3 0.7 copy-start.4
  7.0 0.7 copy-start.5
  7.7 0.7 copy-start.6
  8.4 0.7 copy-start.7

commit v2 on v1

--- a/solution.py
+++ b/solution.py
@@ -45,9 +45,9 @@
 
 
 def kernel(
-    ids_ref, len_ref, gain_ref, a_ref, b_ref, table_hbm, w_hbm, cache_hbm, q_hbm,
+    ids_hbm, len_hbm, gain_hbm, a_hbm, b_hbm, table_hbm, w_hbm, cache_hbm, q_hbm,
     att_ref, kv_ref,
-    table, weight, cache, q_in, load_sem,
+    ids_ref, len_ref, gain_ref, a_ref, b_ref, table, weight, cache, q_in, load_sem,
     ids_one, ids_all, fac_one, fac_all, qs, qbd,
     core_out, core_in, plane_out, plane_in, merged,
     part_out, part_in, stat_out, stat_in, old_all, old_stat,
@@ -85,7 +85,16 @@
         pltpu.make_async_copy(cache_hbm, cache, load_sem.at[1]),
         pltpu.make_async_copy(table_hbm, table, load_sem.at[2]),
         pltpu.make_async_copy(w_hbm, weight, load_sem.at[3]),
+        pltpu.make_async_copy(len_hbm, len_ref, load_sem.at[4]),
+        pltpu.make_async_copy(gain_hbm, gain_ref, load_sem.at[5]),
     ]
+    urgent = [
+        pltpu.make_async_copy(ids_hbm, ids_ref, load_sem.at[6]),
+        pltpu.make_async_copy(a_hbm, a_ref, load_sem.at[7]),
+        pltpu.make_async_copy(b_hbm, b_ref, load_sem.at[8]),
+    ]
+    for load in urgent:
+        load.start()
     for load in loads:
         load.start()
 
@@ -98,6 +107,8 @@
     loop(Y, X * Y, lambda d: hello((rep((x + d // Y) % X, zh, (y + d % Y) % Y, c), t)))
     loop(ZH, ZH * T, lambda d: hello((rep(x, (zh + d % ZH) % ZH, y, c), (t + d // ZH) % T)))
 
+    for load in urgent:
+        load.wait()
     lane = iota((1, LANES), 1)
     row = jnp.zeros((1, LANES), jnp.int32)
     base = (y * ZH + zh) * toks
@@ -143,6 +154,7 @@
         for g in range(KVH):
             qbd[a, g * span : (g + 1) * span, g * HD : (g + 1) * HD] = tall[g * span : (g + 1) * span, :]
     loads[1].wait()
+    loads[4].wait()
     scale = 1.0 / math.sqrt(HD)
 
     def attend(a):
@@ -270,6 +282,7 @@
 
     loop(1, X, lambda d: fa2_in(d).wait_recv())
     loads[3].wait()
+    loads[5].wait()
     for p in range(2):
         full = []
         for side in range(2):
@@ -335,10 +348,12 @@
     embedded = plane_in[0].astype(F32)
     for i in range(1, X * Y):
         embedded = embedded + plane_in[i].astype(F32)
+    gain = gain_ref[...].astype(F32)
+    gain = jnp.concatenate([gain[i : i + 1] for i in range(chunks)], axis=1)
     squares = jnp.sum(embedded * embedded, axis=1, keepdims=True)
     squares = jnp.where(iota((share, LANES), 0) == iota((share, LANES), 1), squares, 0.0)
     sq_out[...] = jnp.sum(squares, axis=0, keepdims=True)
-    ready = (embedded * (gain_ref[...].astype(F32) * SHRINK)).astype(BF16)
+    ready = (embedded * (gain * SHRINK)).astype(BF16)
     proj = [jnp.dot(ready, merged[p], preferred_element_type=F32) for p in range(2)]
     for zh_ in range(ZH):
         for t_ in range(T):
@@ -464,17 +479,21 @@
     rows, steps = ids.shape
     voc, feat = table.shape
     vmem = pl.BlockSpec(memory_space=pltpu.VMEM)
-    smem = pl.BlockSpec(memory_space=pltpu.SMEM)
-    hbm = pl.BlockSpec(memory_space=pl.ANY)
+    hbm = pl.BlockSpec(memory_space=pltpu.HBM)
     share = ZH * rows * steps
     dma = pltpu.SemaphoreType.DMA
     half = LANES // 2
     scratch = [
+        pltpu.SMEM(ids.shape, jnp.int32),
+        pltpu.SMEM(lengths.shape, jnp.int32),
+        pltpu.VMEM((feat // LANES, LANES), BF16),
+        pltpu.VMEM((2, feat), BF16),
+        pltpu.VMEM((2, feat), BF16),
         pltpu.VMEM(table.shape, BF16),
         pltpu.VMEM(weight.shape, BF16),
         pltpu.VMEM(cache.shape, BF16),
         pltpu.VMEM(queries.shape, BF16),
-        dma((4,)),
+        dma((9,)),
         pltpu.VMEM((GROUP, 1, LANES), jnp.int32),
         pltpu.VMEM((X, C, LANES), jnp.int32),
         pltpu.VMEM((GROUP, 16, LANES), BF16),
@@ -508,17 +527,17 @@
             jax.ShapeDtypeStruct((rows, steps, QH * HD), BF16),
             jax.ShapeDtypeStruct((2, rows, steps, KVH * HD), BF16),
         ),
-        in_specs=[smem, smem, vmem, vmem, vmem, hbm, hbm, hbm, hbm],
+        in_specs=[hbm] * 9,
         out_specs=(vmem, vmem),
         scratch_shapes=scratch,
         compiler_params=pltpu.CompilerParams(
-            collective_id=0, has_side_effects=True, vmem_limit_bytes=48 * 1024 * 1024
+            collective_id=0, has_side_effects=True, vmem_limit_bytes=60 * 1024 * 1024
         ),
         cost_estimate=pl.CostEstimate(flops=2_000_000_000, bytes_accessed=5_000_000, transcendentals=200_000),
     )(
         ids,
         lengths,
-        gain.reshape(1, feat),
+        gain.reshape(feat // LANES, LANES),
         in_factor.reshape(2, feat),
         out_factor.reshape(2, feat),
         table,

time: 71.6 us -> 64.2 us (0.90)
  local copies, waits for them, and re-layouts: 9.66 us -> 2.99 us
    unnamed x18 -> x2, local copies, waits for them, and re-layouts: 8.98 us -> 2.99 us
where the time goes in v2:
time: 64.2 us; the launch traced here: 64 us
  Pallas kernels  60.4 us (94%)
  local copies, waits for them, and re-layouts  2.99 us (5%)
    pallas_call x1, Pallas kernels, shards(): pl.pallas_call(kernel, out_shape=(jax.ShapeDtypeStruct((rows, steps, QH *...  60.4 us
    unnamed x2, local copies, waits for them, and re-layouts  2.99 us

profile of v2, /device:TPU:1, one launch (start us, length us, event | category | flops | bytes accessed | tf_op | source)
XLA Modules:
  0.0 64.0 jit_solution(5015928007032816125)
XLA Ops:
  0.6 60.4 %shard_map.104 = (bf16[4,4,4096]{2,1,0:T(4,128)(2,1)}, bf16[2,4,4,512]{3,2,1,0:T(4,128)(2,1)}) custom-call(s32[4,4]{1,0:T(4,128)} %ids_hbm.1, s32[4]{0:T(128)} %len_hbm.1, bf16[4,128]{1,0:T(4,128)(2,1)} %bitcast.5, bf16[2,512]{1,0:T(2,128)(2,1)} %bitcast.3, bf16[2,512]{1,0:T(2,128)(2,1)} %bitcast.4, bf16[1200,512]{1,0:T(8,128)(2,1)} %table_hbm.1, ...), custom_call_target="tpu_custom_call" | custom-call | flops 2000000000 | bytes 5000000 | tf_op jit(solution)/shard_map/pallas_call | solution.py:524
  61.0 1.6 %copy.13 = bf16[4,4,4096]{2,1,0:T(4,128)(2,1)} copy(bf16[4,4,4096]{2,1,0:T(4,128)(2,1)} %get-tuple-element.4) | data formatting | bytes 262144
  62.7 1.4 %copy.14 = bf16[2,4,4,512]{3,2,1,0:T(4,128)(2,1)} copy(bf16[2,4,4,512]{3,2,1,0:T(4,128)(2,1)} %get-tuple-element.5) | data formatting | bytes 65536

commit v3 on v2

--- a/solution.py
+++ b/solution.py
@@ -473,6 +473,11 @@
     loop(1, ZH * T, lambda d: sq(d).wait_send())
     loop(1, ZH * T, lambda d: kv(d).wait_send())
     loop(1, T, lambda d: new(d).wait_send())
+
+
+def deliver(att_in, kv_in, att_out, kv_out):
+    att_out[...] = att_in[...]
+    kv_out[...] = kv_in[...]
 
 
 def shards(ids, table, gain, weight, in_factor, out_factor, cache, lengths, queries):
@@ -521,7 +526,7 @@
         scratch.append(dma((count,)))
     for count in (T, T, T, T, ZH * T, ZH * T, ZH * T, ZH * T, T, T):
         scratch.append(dma((count,)))
-    return pl.pallas_call(
+    made = pl.pallas_call(
         kernel,
         out_shape=(
             jax.ShapeDtypeStruct((rows, steps, QH * HD), BF16),
@@ -545,6 +550,13 @@
         cache,
         queries,
     )
+    return pl.pallas_call(
+        deliver,
+        out_shape=tuple(jax.ShapeDtypeStruct(one.shape, one.dtype) for one in made),
+        in_specs=[vmem, vmem],
+        out_specs=(vmem, vmem),
+        compiler_params=pltpu.CompilerParams(vmem_limit_bytes=60 * 1024 * 1024),
+    )(*made)
 
 
 def solution(mesh):

time: 64.2 us -> 62.8 us (0.978)
  local copies, waits for them, and re-layouts: 2.99 us -> 0 us
  Pallas kernels: 60.4 us -> 62 us
    unnamed x2 -> x0, local copies, waits for them, and re-layouts: 2.99 us -> none
    pallas_call x0 -> x1, Pallas kernels: none -> 1.57 us  [shards(): pl.pallas_call(deliver, out_shape=tuple((jax.ShapeDtypeStruct(one.shape,...]
where the time goes in v3:
time: 62.8 us; the launch traced here: 62.6 us
  Pallas kernels  62 us (99%)
  between operations  0.64 us (1%)
    pallas_call x1, Pallas kernels, shards(): pl.pallas_call(kernel, out_shape=(jax.ShapeDtypeStruct((rows, steps, QH *...  60.4 us
    pallas_call x1, Pallas kernels, shards(): pl.pallas_call(deliver, out_shape=tuple((jax.ShapeDtypeStruct(one.shape,...  1.57 us

profile of v3, /device:TPU:1, one launch (start us, length us, event | category | flops | bytes accessed | tf_op | source)
XLA Modules:
  0.0 62.6 jit_solution(5726592417521880511)
XLA Ops:
  0.6 60.4 %shard_map.104 = (bf16[4,4,4096]{2,1,0:T(4,128)(2,1)}, bf16[2,4,4,512]{3,2,1,0:T(4,128)(2,1)}) custom-call(s32[4,4]{1,0:T(4,128)} %ids_hbm.1, s32[4]{0:T(128)} %len_hbm.1, bf16[4,128]{1,0:T(4,128)(2,1)} %bitcast.5, bf16[2,512]{1,0:T(2,128)(2,1)} %bitcast.3, bf16[2,512]{1,0:T(2,128)(2,1)} %bitcast.4, bf16[1200,512]{1,0:T(8,128)(2,1)} %table_hbm.1, ...), custom_call_target="tpu_custom_call" | custom-call | flops 2000000000 | bytes 5000000 | tf_op jit(solution)/shard_map/pallas_call | solution.py:529
  61.0 1.6 %shard_map.105 = (bf16[4,4,4096]{2,1,0:T(4,128)(2,1)}, bf16[2,4,4,512]{3,2,1,0:T(4,128)(2,1)}) custom-call(bf16[4,4,4096]{2,1,0:T(4,128)(2,1)} %get-tuple-element.4.att_in, bf16[2,4,4,512]{3,2,1,0:T(4,128)(2,1)} %get-tuple-element.5.kv_in), custom_call_target="tpu_custom_call" | custom-call | tf_op jit(solution)/shard_map/pallas_call | solution.py:553
